TPU v7x, 32 devices: a whole 2x2x4 slice. The times are simulated.
32 devices in a mesh: vol: 16 (over z, y, core), strip: 2 (over x).
Axes of the slice: x: 2, y: 2, z: 4, core: 2. Of those that a mesh axis runs over, the one named last changes fastest.
Arguments:
- frames: bfloat16 [32, 1, 128, 1024], P('vol', None, 'strip'), may hold values from 0.5 to 4
- kappa: float32 [32], P('vol'), may hold values from 0.3 to 3
Outputs:
- dff: bfloat16 [32, 1, 64, 2, 1024], P(None, None, 'vol', 'strip')
- slope: bfloat16 [32, 1, 64, 2, 1024], P(None, None, 'vol', 'strip')
All inputs are finite; a program needn't handle non-finite values.
Results may differ from a plain program's by a relative error of at most 0.0097.
Values may be sent and summed in bfloat16 or wider, within the bound.
A program may use at most 64 MiB of HBM per device.

v0:
```python
import functools

import jax
import jax.numpy as jnp
from jax import lax
from jax.experimental import pallas as pl
from jax.experimental.pallas import tpu as pltpu
from jax.sharding import PartitionSpec as P

PASSES = 3
BAND = 16
LANES = 128
TILE = 8
PACK = 16
MESH = pl.DeviceIdType.MESH


def inverse(value):
    guess = pltpu.reciprocal(value, approx=True)
    return guess * (2.0 - value * guess)


def flux(diff):
    return diff * inverse(1.0 + diff * diff)


def shifted_rows(center, below):
    row = lax.broadcasted_iota(jnp.int32, center.shape, 0)
    return pltpu.roll(jnp.where(row == 0, below, center), TILE - 1, 0)


def flux_x(center):
    nx = center.shape[1]
    lane = lax.broadcasted_iota(jnp.int32, (TILE, LANES), 1)
    left = pltpu.roll(center, 1, 1)
    left = jnp.concatenate([jnp.where(lane == 0, 0.0, left[:, :LANES]), left[:, LANES:]], axis=1)
    into = flux(left - center)
    out = pltpu.roll(into, nx - 1, 1)
    edge = flux(center[:, nx - LANES :])
    out = jnp.concatenate([out[:, : nx - LANES], jnp.where(lane == LANES - 1, edge, out[:, nx - LANES :])], axis=1)
    return into - out


def advance(tiles, emit):
    count = len(tiles)
    center = tiles[0]()
    zero = jnp.zeros_like(center)
    row = lax.broadcasted_iota(jnp.int32, center.shape, 0)
    before = flux(shifted_rows(zero, center))
    for i in range(count):
        below = tiles[i + 1]() if i + 1 < count else zero
        down = flux(shifted_rows(center, below) - center)
        up = pltpu.roll(jnp.where(row == TILE - 1, before, down), 1, 0)
        total = (down - up) + flux_x(center)
        emit(i, center + 0.2 * total)
        before, center = down, below


def folded(value, lower):
    small = lax.broadcasted_iota(jnp.int32, (TILE, LANES), 0) < TILE // 2
    swapped = pltpu.roll(value, TILE // 2, 0)
    first, second = (swapped, value) if lower else (value, swapped)
    parts = []
    for c in range(0, value.shape[1], 2 * LANES):
        parts.append(jnp.where(small, first[:, c : c + LANES], second[:, c + LANES : c + 2 * LANES]))
    return jnp.concatenate(parts, axis=0).astype(jnp.bfloat16)


def kernel(n, strips, frames, kappa, dff, slope, held, kap, halo, field, send, recv, mix, ratio,
           load_sem, halo_send, halo_recv, send_sem, recv_sem, own_sem):
    vols, _, rows, nx = frames.shape
    times, depth, _ = recv.shape
    tiles = rows // TILE
    me = lax.axis_index("vol")
    strip = lax.axis_index("strip")
    has_up = strip > 0
    has_down = strip < strips - 1

    loads = [pltpu.make_async_copy(frames.at[v, 0], held.at[v], load_sem.at[v]) for v in range(vols)]
    load_kappa = pltpu.make_async_copy(kappa, kap, load_sem.at[vols])
    load_kappa.start()
    for load in loads:
        load.start()

    barrier = pltpu.get_barrier_semaphore()

    @pl.loop(1, n)
    def _(k):
        pl.semaphore_signal(barrier, inc=1, device_id={"vol": lax.rem(me + k, n)}, device_id_type=MESH)

    @pl.when(has_up)
    def _():
        pl.semaphore_signal(barrier, inc=1, device_id={"strip": strip - 1}, device_id_type=MESH)

    @pl.when(has_down)
    def _():
        pl.semaphore_signal(barrier, inc=1, device_id={"strip": strip + 1}, device_id_type=MESH)

    def to_up():
        return pltpu.make_async_remote_copy(
            src_ref=frames.at[:, 0, pl.ds(0, PACK)], dst_ref=halo.at[1],
            send_sem=halo_send.at[1], recv_sem=halo_recv.at[1],
            device_id={"strip": strip - 1}, device_id_type=MESH)

    def to_down():
        return pltpu.make_async_remote_copy(
            src_ref=frames.at[:, 0, pl.ds(rows - PACK, PACK)], dst_ref=halo.at[0],
            send_sem=halo_send.at[0], recv_sem=halo_recv.at[0],
            device_id={"strip": strip + 1}, device_id_type=MESH)

    parts = depth // PACK
    pieces = [(v, 0, depth) for v in range(vols - 1)] + [(vols - 1, p * PACK, PACK) for p in range(parts)]

    def sending(v, start, length, piece, to):
        return pltpu.make_async_remote_copy(
            src_ref=send.at[v, to, pl.ds(start, length)], dst_ref=recv.at[me * vols + v, pl.ds(start, length)],
            send_sem=send_sem.at[piece], recv_sem=recv_sem.at[piece],
            device_id={"vol": to}, device_id_type=MESH)

    def all_of(piece):
        _, start, length = pieces[piece]
        return pltpu.make_async_remote_copy(
            src_ref=send.at[0, pl.ds(0, n - 1), pl.ds(start, length)], dst_ref=recv.at[pl.ds(0, n - 1), pl.ds(start, length)],
            send_sem=send_sem.at[piece], recv_sem=recv_sem.at[piece],
            device_id={"vol": lax.rem(me + 1, n)}, device_id_type=MESH)

    def scaled(block, v):
        return block.astype(jnp.float32) * (1.0 / jnp.full(block.shape, kap[v], jnp.float32))

    def getters(v, step):
        if step == 0:
            cache = {}

            def get(i):
                if i // 2 not in cache:
                    cache[i // 2] = scaled(held[v, (i // 2) * PACK : (i // 2 + 1) * PACK, :], v)
                return cache[i // 2][i % 2 * TILE : i % 2 * TILE + TILE]
        else:
            def get(i):
                return field[(step - 1) % 2, i * TILE : (i + 1) * TILE, :]
        return [functools.partial(get, i) for i in range(tiles)]

    def order(body):
        def step(j, _):
            away = (j + 1) // 2
            body(lax.rem(me + n // 2 + n + jnp.where(j % 2 == 1, away, -away), n))
            return _

        lax.fori_loop(0, n - 1, step, 0, unroll=n <= 16)

    load_kappa.wait()

    @pl.loop(0, vols)
    def _(v):
        pltpu.make_async_copy(frames.at[v, 0], held.at[v], load_sem.at[v]).wait()
        unscale = jnp.full((TILE, nx), kap[v], jnp.float32)
        for step in range(PASSES):
            def emit(i, value, step=step):
                if step < PASSES - 1:
                    field[step % 2, i * TILE : (i + 1) * TILE, :] = value
                else:
                    value = value * unscale
                    send[v, 2 * i] = folded(value, False)
                    send[v, 2 * i + 1] = folded(value, True)

            advance(getters(v, step), emit)

        @pl.when(v == 0)
        def _():
            pl.semaphore_wait(barrier, n - 1 + has_up.astype(jnp.int32) + has_down.astype(jnp.int32))

            @pl.when(has_up)
            def _():
                to_up().start()

            @pl.when(has_down)
            def _():
                to_down().start()

        @pl.when(v < vols - 1)
        def _():
            def whole(to):
                @pl.when(jnp.logical_and(to > 0, to < n - 1))
                def _():
                    sending(v, 0, depth, v, to).start()

            order(whole)

        @pl.when(v == vols - 1)
        def _():
            for p in range(parts):
                def part(to):
                    @pl.when(jnp.logical_and(to > 0, to < n - 1))
                    def _():
                        sending(v, p * PACK, PACK, vols - 1 + p, to).start()

                order(part)

    def edge(own, other, own_first, v):
        both = [own, other] if own_first else [other, own]
        for step in range(PASSES):
            made = []
            advance([lambda x=x: x for x in both], lambda i, value: made.append(value))
            both = made
        return both[0 if own_first else 1] * jnp.full(own.shape, kap[v], jnp.float32)

    @pl.when(has_up)
    def _():
        to_down().wait_recv()
        @pl.loop(0, vols)
        def _(v):
            beyond = scaled(halo[0, v], v)[PACK - TILE :]
            mine = scaled(held[v, :PACK, :], v)[:TILE]
            send[v, 0] = folded(edge(mine, beyond, False, v), False)

    @pl.when(has_down)
    def _():
        to_up().wait_recv()
        @pl.loop(0, vols)
        def _(v):
            beyond = scaled(halo[1, v], v)[:TILE]
            mine = scaled(held[v, rows - PACK : rows, :], v)[PACK - TILE :]
            send[v, n - 1] = folded(edge(mine, beyond, True, v), True)

    for to in (0, n - 1):
        @pl.when(me != to)
        def _():
            for piece in range(len(pieces)):
                sending(*pieces[piece], piece, to).start()

    own = [pltpu.make_async_copy(send.at[v, me], recv.at[me * vols + v], own_sem.at[v]) for v in range(vols)]
    for copy in own:
        copy.start()

    column = lax.broadcasted_iota(jnp.int32, (PACK, times * PACK), 1)
    diagonal = column % PACK == lax.broadcasted_iota(jnp.int32, (PACK, times * PACK), 0)
    source = column // PACK

    @pl.loop(0, times)
    def _(t):
        ahead = jnp.maximum(BAND - t, 0)
        behind = jnp.maximum(t + BAND + 1 - times, 0)
        total = (BAND + 1) ** 2 - (ahead * (ahead + 1) + behind * (behind + 1)) // 2
        raw = jnp.maximum(BAND + 1 - jnp.abs(source - t), 0).astype(jnp.float32)
        weight = raw / jnp.full(raw.shape, total, jnp.int32).astype(jnp.float32)
        mix[pl.ds(pl.multiple_of(t * PACK, PACK), PACK), :] = jnp.where(diagonal, weight, 0.0).astype(jnp.bfloat16)

    for copy in own:
        copy.wait()
    for piece in range(vols - 1):
        all_of(piece).wait_recv()

    block = min(times, 32)
    for p in range(parts):
        all_of(vols - 1 + p).wait_recv()
        span = slice(p * PACK, (p + 1) * PACK)
        values = recv[:, span, :].reshape(times * PACK, LANES)
        for start in range(0, times, block):
            these = pl.ds(start, block)
            base = jnp.dot(mix[start * PACK : (start + block) * PACK, :], values, preferred_element_type=jnp.float32)
            base = base.reshape(block, PACK, LANES)
            got = (recv[these, span, :].astype(jnp.float32) - base) * inverse(base + 0.1)
            ratio[these, span, :] = got
            dff[these, span, :] = got.astype(jnp.bfloat16)
        slope[0, span] = (ratio[1, span] - ratio[0, span]).astype(jnp.bfloat16)
        slope[1 : times - 1, span] = ((ratio[2:, span] - ratio[: times - 2, span]) * 0.5).astype(jnp.bfloat16)
        slope[times - 1, span] = (ratio[times - 1, span] - ratio[times - 2, span]).astype(jnp.bfloat16)

    for piece in range(len(pieces)):
        all_of(piece).wait_send()

    @pl.when(has_up)
    def _():
        to_up().wait_send()

    @pl.when(has_down)
    def _():
        to_down().wait_send()


def leave(dff, slope, dff_out, slope_out, sem):
    half = dff.shape[0] // 2
    copies = [
        pltpu.make_async_copy(source.at[pl.ds(h * half, half)], target.at[pl.ds(h * half, half)], sem.at[k, h])
        for k, (source, target) in enumerate(((dff, dff_out), (slope, slope_out)))
        for h in range(2)
    ]
    for copy in copies:
        copy.start()
    for copy in copies:
        copy.wait()


def local(n, strips, frames, kappa):
    vols, planes, rows, nx = frames.shape
    times = vols * n
    each = rows // n
    assert planes == 1 and each * 2 == TILE and nx % (2 * LANES) == 0
    depth = each * nx // LANES
    pieces = vols - 1 + depth // PACK
    out = jax.ShapeDtypeStruct((times, depth, LANES), jnp.bfloat16)
    f32, bf16 = jnp.float32, jnp.bfloat16
    results = pl.pallas_call(
        functools.partial(kernel, n, strips),
        out_shape=(out, out),
        in_specs=[pl.BlockSpec(memory_space=pltpu.HBM)] * 2,
        out_specs=(pl.BlockSpec(memory_space=pltpu.VMEM),) * 2,
        scratch_shapes=[
            pltpu.VMEM((vols, rows, nx), bf16),
            pltpu.SMEM((vols,), f32),
            pltpu.VMEM((2, vols, PACK, nx), bf16),
            pltpu.VMEM((2, rows, nx), f32),
            pltpu.VMEM((vols, n, depth, LANES), bf16),
            pltpu.VMEM((times, depth, LANES), bf16),
            pltpu.VMEM((times * PACK, times * PACK), bf16),
            pltpu.VMEM((times, depth, LANES), f32),
            pltpu.SemaphoreType.DMA((vols + 1,)),
            pltpu.SemaphoreType.DMA((2,)),
            pltpu.SemaphoreType.DMA((2,)),
            pltpu.SemaphoreType.DMA((pieces,)),
            pltpu.SemaphoreType.DMA((pieces,)),
            pltpu.SemaphoreType.DMA((vols,)),
        ],
        compiler_params=pltpu.CompilerParams(
            collective_id=0, has_side_effects=True, vmem_limit_bytes=40 * 1024 * 1024),
        cost_estimate=pl.CostEstimate(flops=200_000_000, bytes_accessed=1_000_000, transcendentals=1_000_000),
    )(pltpu.with_memory_space_constraint(frames, pltpu.HBM), pltpu.with_memory_space_constraint(kappa, pltpu.HBM))

    results = pl.pallas_call(
        leave,
        out_shape=(out, out),
        in_specs=[pl.BlockSpec(memory_space=pl.ANY)] * 2,
        out_specs=(pl.BlockSpec(memory_space=pltpu.HBM),) * 2,
        scratch_shapes=[pltpu.SemaphoreType.DMA((2, 2))],
        cost_estimate=pl.CostEstimate(flops=0, bytes_accessed=1_000_000, transcendentals=0),
    )(*results)

    def laid(value):
        value = value.reshape(times, nx // LANES, each, LANES).transpose(0, 2, 1, 3)
        return value.reshape(times, 1, each, 1, nx)

    return laid(results[0]), laid(results[1])


def solution(mesh):
    placed = P(None, None, "vol", "strip", None)
    return jax.shard_map(
        functools.partial(local, mesh.shape["vol"], mesh.shape["strip"]),
        mesh=mesh,
        in_specs=(P("vol", None, "strip", None), P("vol")),
        out_specs=(placed, placed),
        check_vma=False,
    )
```

profile of v0, /device:TPU:0, one launch (start us, length us, event | category | flops | bytes accessed | tf_op | source)
XLA Modules:
  0.0 34.5 jit_solution(2040249496640134082)
XLA Ops:
  0.6 15.5 %shard_map.41 = (bf16[32,32,128]{2,1,0:T(8,128)(2,1)S(1)}, bf16[32,32,128]{2,1,0:T(8,128)(2,1)S(1)}) custom-call(bf16[2,1,64,1024]{3,2,1,0:T(8,128)(2,1)} %frames.1, f32[2]{0:T(128)} %kappa.1), custom_call_target="tpu_custom_call" | custom-call | flops 200000000 | bytes 1000000 | tf_op jit(solution)/shard_map/pallas_call | solution.py:303
  16.1 0.0 copy-start
  16.1 0.7 %copy-done = bf16[32,32,128]{2,1,0:T(8,128)(2,1)} copy-done((bf16[32,32,128]{2,1,0:T(8,128)(2,1)}, bf16[32,32,128]{2,1,0:T(8,128)(2,1)S(1)}, u32[]{:S(2)}) %copy-start) | copy-done | bytes 262168
  16.8 0.0 copy-start.1
  16.8 0.7 %copy-done.1 = bf16[32,32,128]{2,1,0:T(8,128)(2,1)} copy-done((bf16[32,32,128]{2,1,0:T(8,128)(2,1)}, bf16[32,32,128]{2,1,0:T(8,128)(2,1)S(1)}, u32[]{:S(2)}) %copy-start.1) | copy-done | bytes 262168
  17.5 17.0 %shard_map.42 = (bf16[32,32,128]{2,1,0:T(8,128)(2,1)}, bf16[32,32,128]{2,1,0:T(8,128)(2,1)}) custom-call(bf16[32,32,128]{2,1,0:T(8,128)(2,1)} %copy-done, bf16[32,32,128]{2,1,0:T(8,128)(2,1)} %copy-done.1), custom_call_target="tpu_custom_call" | custom-call | bytes 1000000 | tf_op jit(solution)/shard_map/pallas_call | solution.py:329
Async XLA Ops:
  16.1 0.7 %copy-start = (bf16[32,32,128]{2,1,0:T(8,128)(2,1)}, bf16[32,32,128]{2,1,0:T(8,128)(2,1)S(1)}, u32[]{:S(2)}) copy-start(bf16[32,32,128]{2,1,0:T(8,128)(2,1)S(1)} %get-tuple-element.6.dff) | copy-start | bytes 786436
  16.8 0.7 %copy-start.1 = (bf16[32,32,128]{2,1,0:T(8,128)(2,1)}, bf16[32,32,128]{2,1,0:T(8,128)(2,1)S(1)}, u32[]{:S(2)}) copy-start(bf16[32,32,128]{2,1,0:T(8,128)(2,1)S(1)} %get-tuple-element.7.slope) | copy-start | bytes 786436
where the time goes:
time: 34.7 us; the launch traced here: 34.5 us
  Pallas kernels  32.5 us (94%)
  local copies, waits for them, and re-layouts  1.37 us (4%)
  between operations  0.65 us (2%)
    pallas_call x1, Pallas kernels, local(): pl.pallas_call(leave, out_shape=(out, out), in_specs=[pl.BlockSpec(memory...  17 us
    pallas_call x1, Pallas kernels, local(): pl.pallas_call(functools.partial(kernel, n, strips), out_shape=(out, out)...  15.5 us
    unnamed x4, local copies, waits for them, and re-layouts  1.37 us

commit v1 on v0

--- a/solution.py
+++ b/solution.py
@@ -66,7 +66,7 @@
     return jnp.concatenate(parts, axis=0).astype(jnp.bfloat16)
 
 
-def kernel(n, strips, frames, kappa, dff, slope, held, kap, halo, field, send, recv, mix, ratio,
+def kernel(n, strips, frames, kappa, dff, slope, held, kap, rim, halo, beyond, field, send, recv, mix, ratio,
            load_sem, halo_send, halo_recv, send_sem, recv_sem, own_sem):
     vols, _, rows, nx = frames.shape
     times, depth, _ = recv.shape
@@ -98,14 +98,12 @@
 
     def to_up():
         return pltpu.make_async_remote_copy(
-            src_ref=frames.at[:, 0, pl.ds(0, PACK)], dst_ref=halo.at[1],
-            send_sem=halo_send.at[1], recv_sem=halo_recv.at[1],
+            src_ref=rim.at[1], dst_ref=halo.at[1], send_sem=halo_send.at[1], recv_sem=halo_recv.at[1],
             device_id={"strip": strip - 1}, device_id_type=MESH)
 
     def to_down():
         return pltpu.make_async_remote_copy(
-            src_ref=frames.at[:, 0, pl.ds(rows - PACK, PACK)], dst_ref=halo.at[0],
-            send_sem=halo_send.at[0], recv_sem=halo_recv.at[0],
+            src_ref=rim.at[0], dst_ref=halo.at[0], send_sem=halo_send.at[0], recv_sem=halo_recv.at[0],
             device_id={"strip": strip + 1}, device_id_type=MESH)
 
     parts = depth // PACK
@@ -140,6 +138,10 @@
                 return field[(step - 1) % 2, i * TILE : (i + 1) * TILE, :]
         return [functools.partial(get, i) for i in range(tiles)]
 
+    def ready(to):
+        return jnp.logical_not(jnp.logical_or(
+            jnp.logical_and(has_up, to == 0), jnp.logical_and(has_down, to == n - 1)))
+
     def order(body):
         def step(j, _):
             away = (j + 1) // 2
@@ -150,9 +152,17 @@
 
     load_kappa.wait()
 
+    for load in loads:
+        load.wait()
+
+    f32 = jnp.float32
+    rim[1] = jnp.concatenate(
+        [held[v, :PACK, :].astype(f32)[:TILE] for v in range(vols)], axis=0).astype(jnp.bfloat16)
+    rim[0] = jnp.concatenate(
+        [held[v, rows - PACK :, :].astype(f32)[TILE:] for v in range(vols)], axis=0).astype(jnp.bfloat16)
+
     @pl.loop(0, vols)
     def _(v):
-        pltpu.make_async_copy(frames.at[v, 0], held.at[v], load_sem.at[v]).wait()
         unscale = jnp.full((TILE, nx), kap[v], jnp.float32)
         for step in range(PASSES):
             def emit(i, value, step=step):
@@ -165,22 +175,23 @@
 
             advance(getters(v, step), emit)
 
-        @pl.when(v == 0)
-        def _():
-            pl.semaphore_wait(barrier, n - 1 + has_up.astype(jnp.int32) + has_down.astype(jnp.int32))
-
-            @pl.when(has_up)
-            def _():
-                to_up().start()
-
-            @pl.when(has_down)
-            def _():
-                to_down().start()
+            if step == 0:
+                @pl.when(v == 0)
+                def _():
+                    pl.semaphore_wait(barrier, n - 1 + has_up.astype(jnp.int32) + has_down.astype(jnp.int32))
+
+                    @pl.when(has_up)
+                    def _():
+                        to_up().start()
+
+                    @pl.when(has_down)
+                    def _():
+                        to_down().start()
 
         @pl.when(v < vols - 1)
         def _():
             def whole(to):
-                @pl.when(jnp.logical_and(to > 0, to < n - 1))
+                @pl.when(ready(to))
                 def _():
                     sending(v, 0, depth, v, to).start()
 
@@ -190,7 +201,7 @@
         def _():
             for p in range(parts):
                 def part(to):
-                    @pl.when(jnp.logical_and(to > 0, to < n - 1))
+                    @pl.when(ready(to))
                     def _():
                         sending(v, p * PACK, PACK, vols - 1 + p, to).start()
 
@@ -204,29 +215,33 @@
             both = made
         return both[0 if own_first else 1] * jnp.full(own.shape, kap[v], jnp.float32)
 
-    @pl.when(has_up)
-    def _():
-        to_down().wait_recv()
+    def edges(to, copy, which, own_first):
+        copy.wait_recv()
+        got = halo[which].astype(f32)
+        for v in range(vols):
+            beyond[v] = got[v * TILE : (v + 1) * TILE]
+
         @pl.loop(0, vols)
         def _(v):
-            beyond = scaled(halo[0, v], v)[PACK - TILE :]
-            mine = scaled(held[v, :PACK, :], v)[:TILE]
-            send[v, 0] = folded(edge(mine, beyond, False, v), False)
-
-    @pl.when(has_down)
-    def _():
-        to_up().wait_recv()
-        @pl.loop(0, vols)
-        def _(v):
-            beyond = scaled(halo[1, v], v)[:TILE]
-            mine = scaled(held[v, rows - PACK : rows, :], v)[PACK - TILE :]
-            send[v, n - 1] = folded(edge(mine, beyond, True, v), True)
-
-    for to in (0, n - 1):
+            other = scaled(beyond[v], v)
+            if own_first:
+                mine = scaled(held[v, rows - PACK : rows, :], v)[TILE:]
+            else:
+                mine = scaled(held[v, :PACK, :], v)[:TILE]
+            send[v, to] = folded(edge(mine, other, own_first, v), own_first)
+
         @pl.when(me != to)
         def _():
             for piece in range(len(pieces)):
                 sending(*pieces[piece], piece, to).start()
+
+    @pl.when(has_up)
+    def _():
+        edges(0, to_down(), 0, False)
+
+    @pl.when(has_down)
+    def _():
+        edges(n - 1, to_up(), 1, True)
 
     own = [pltpu.make_async_copy(send.at[v, me], recv.at[me * vols + v], own_sem.at[v]) for v in range(vols)]
     for copy in own:
@@ -308,7 +323,9 @@
         scratch_shapes=[
             pltpu.VMEM((vols, rows, nx), bf16),
             pltpu.SMEM((vols,), f32),
-            pltpu.VMEM((2, vols, PACK, nx), bf16),
+            pltpu.VMEM((2, vols * TILE, nx), bf16),
+            pltpu.VMEM((2, vols * TILE, nx), bf16),
+            pltpu.VMEM((vols, TILE, nx), f32),
             pltpu.VMEM((2, rows, nx), f32),
             pltpu.VMEM((vols, n, depth, LANES), bf16),
             pltpu.VMEM((times, depth, LANES), bf16),
@@ -332,8 +349,9 @@
         in_specs=[pl.BlockSpec(memory_space=pl.ANY)] * 2,
         out_specs=(pl.BlockSpec(memory_space=pltpu.HBM),) * 2,
         scratch_shapes=[pltpu.SemaphoreType.DMA((2, 2))],
+        compiler_params=pltpu.CompilerParams(vmem_limit_bytes=2 * 1024 * 1024),
         cost_estimate=pl.CostEstimate(flops=0, bytes_accessed=1_000_000, transcendentals=0),
-    )(*results)
+    )(*[pltpu.with_memory_space_constraint(x, pltpu.VMEM) for x in results])
 
     def laid(value):
         value = value.reshape(times, nx // LANES, each, LANES).transpose(0, 2, 1, 3)

time: 34.7 us -> 16.1 us (0.46)
  Pallas kernels: 32.5 us -> 15.3 us
  local copies, waits for them, and re-layouts: 1.37 us -> 0 us
    pallas_call x1, Pallas kernels: 17 us -> 0.82 us  [local(): pl.pallas_call(leave, out_shape=(out, out), in_specs=[pl.BlockSpec(memory...]
    unnamed x4 -> x0, local copies, waits for them, and re-layouts: 1.37 us -> none
    pallas_call x1, Pallas kernels: 15.5 us -> 14.5 us  [local(): pl.pallas_call(functools.partial(kernel, n, strips), out_shape=(out, out)...]
where the time goes in v1:
time: 16.1 us; the launch traced here: 16 us
  Pallas kernels  15.3 us (95%)
  between operations  0.64 us (4%)
    pallas_call x1, Pallas kernels, local(): pl.pallas_call(functools.partial(kernel, n, strips), out_shape=(out, out)...  14.5 us
    pallas_call x1, Pallas kernels, local(): pl.pallas_call(leave, out_shape=(out, out), in_specs=[pl.BlockSpec(memory...  0.82 us

profile of v1, /device:TPU:0, one launch (start us, length us, event | category | flops | bytes accessed | tf_op | source)
XLA Modules:
  0.0 16.0 jit_solution(7936650814041746449)
XLA Ops:
  0.6 14.5 %shard_map.41 = (bf16[32,32,128]{2,1,0:T(8,128)(2,1)S(1)}, bf16[32,32,128]{2,1,0:T(8,128)(2,1)S(1)}) custom-call(bf16[2,1,64,1024]{3,2,1,0:T(8,128)(2,1)} %frames.1, f32[2]{0:T(128)} %kappa.1), custom_call_target="tpu_custom_call" | custom-call | flops 200000000 | bytes 1000000 | tf_op jit(solution)/shard_map/pallas_call | solution.py:318
  15.1 0.8 %shard_map.42 = (bf16[32,32,128]{2,1,0:T(8,128)(2,1)}, bf16[32,32,128]{2,1,0:T(8,128)(2,1)}) custom-call(bf16[32,32,128]{2,1,0:T(8,128)(2,1)S(1)} %get-tuple-element.6.dff, bf16[32,32,128]{2,1,0:T(8,128)(2,1)S(1)} %get-tuple-element.7.slope), custom_call_target="tpu_custom_call" | custom-call | bytes 1000000 | tf_op jit(solution)/shard_map/pallas_call | solution.py:346

commit v2 on v1

--- a/solution.py
+++ b/solution.py
@@ -41,19 +41,18 @@
     return into - out
 
 
-def advance(tiles, emit):
-    count = len(tiles)
+def advance(above, tiles, below, emit):
     center = tiles[0]()
-    zero = jnp.zeros_like(center)
     row = lax.broadcasted_iota(jnp.int32, center.shape, 0)
-    before = flux(shifted_rows(zero, center))
-    for i in range(count):
-        below = tiles[i + 1]() if i + 1 < count else zero
-        down = flux(shifted_rows(center, below) - center)
+    before = above()
+    before = flux(shifted_rows(before, center) - before)
+    for i in range(len(tiles)):
+        after = tiles[i + 1]() if i + 1 < len(tiles) else below()
+        down = flux(shifted_rows(center, after) - center)
         up = pltpu.roll(jnp.where(row == TILE - 1, before, down), 1, 0)
         total = (down - up) + flux_x(center)
         emit(i, center + 0.2 * total)
-        before, center = down, below
+        before, center = down, after
 
 
 def folded(value, lower):
@@ -66,7 +65,7 @@
     return jnp.concatenate(parts, axis=0).astype(jnp.bfloat16)
 
 
-def kernel(n, strips, frames, kappa, dff, slope, held, kap, rim, halo, beyond, field, send, recv, mix, ratio,
+def kernel(n, strips, frames, kappa, dff, slope, held, kap, rim, halo, beyond, start, field, send, recv, mix, ratio,
            load_sem, halo_send, halo_recv, send_sem, recv_sem, own_sem):
     vols, _, rows, nx = frames.shape
     times, depth, _ = recv.shape
@@ -107,7 +106,9 @@
             device_id={"strip": strip + 1}, device_id_type=MESH)
 
     parts = depth // PACK
-    pieces = [(v, 0, depth) for v in range(vols - 1)] + [(vols - 1, p * PACK, PACK) for p in range(parts)]
+    group = n // 2
+    side = me // group
+    near, first_part = vols - 1, vols
 
     def sending(v, start, length, piece, to):
         return pltpu.make_async_remote_copy(
@@ -116,42 +117,39 @@
             device_id={"vol": to}, device_id_type=MESH)
 
     def all_of(piece):
-        _, start, length = pieces[piece]
+        count, length = n - 1, depth
+        if piece == near:
+            count = group - 1
+        elif piece >= first_part:
+            count, length = group, PACK
         return pltpu.make_async_remote_copy(
-            src_ref=send.at[0, pl.ds(0, n - 1), pl.ds(start, length)], dst_ref=recv.at[pl.ds(0, n - 1), pl.ds(start, length)],
+            src_ref=send.at[0, pl.ds(0, count), pl.ds(0, length)], dst_ref=recv.at[pl.ds(0, count), pl.ds(0, length)],
             send_sem=send_sem.at[piece], recv_sem=recv_sem.at[piece],
             device_id={"vol": lax.rem(me + 1, n)}, device_id_type=MESH)
 
     def scaled(block, v):
         return block.astype(jnp.float32) * (1.0 / jnp.full(block.shape, kap[v], jnp.float32))
 
-    def getters(v, step):
-        if step == 0:
-            cache = {}
-
-            def get(i):
-                if i // 2 not in cache:
-                    cache[i // 2] = scaled(held[v, (i // 2) * PACK : (i // 2 + 1) * PACK, :], v)
-                return cache[i // 2][i % 2 * TILE : i % 2 * TILE + TILE]
-        else:
-            def get(i):
-                return field[(step - 1) % 2, i * TILE : (i + 1) * TILE, :]
-        return [functools.partial(get, i) for i in range(tiles)]
+    def tile(ref, i):
+        return ref[pl.ds(pl.multiple_of(i * TILE, TILE), TILE), :]
+
+    def getters(ref, start, count):
+        return [functools.partial(tile, ref, start + i) for i in range(count)]
 
     def ready(to):
         return jnp.logical_not(jnp.logical_or(
-            jnp.logical_and(has_up, to == 0), jnp.logical_and(has_down, to == n - 1)))
-
-    def order(body):
-        def step(j, _):
-            away = (j + 1) // 2
-            body(lax.rem(me + n // 2 + n + jnp.where(j % 2 == 1, away, -away), n))
-            return _
-
-        lax.fori_loop(0, n - 1, step, 0, unroll=n <= 16)
+            jnp.logical_or(jnp.logical_and(has_up, to == 0), jnp.logical_and(has_down, to == n - 1)), to == me))
+
+    zero = jnp.zeros((TILE, nx), jnp.float32)
+    some = tiles // 2
+    for buffer in (0, 1):
+        field[buffer, :TILE, :] = zero
+        field[buffer, (some + 2) * TILE :, :] = zero
+    for v in range(vols):
+        start[v, :TILE, :] = zero
+        start[v, (tiles + 1) * TILE :, :] = zero
 
     load_kappa.wait()
-
     for load in loads:
         load.wait()
 
@@ -160,58 +158,78 @@
         [held[v, :PACK, :].astype(f32)[:TILE] for v in range(vols)], axis=0).astype(jnp.bfloat16)
     rim[0] = jnp.concatenate(
         [held[v, rows - PACK :, :].astype(f32)[TILE:] for v in range(vols)], axis=0).astype(jnp.bfloat16)
-
-    @pl.loop(0, vols)
-    def _(v):
+    for v in range(vols):
+        for i in range(rows // PACK):
+            start[v, TILE + i * PACK : TILE + (i + 1) * PACK, :] = scaled(held[v, i * PACK : (i + 1) * PACK, :], v)
+
+    @pl.loop(0, 2 * vols)
+    def _(unit):
+        v = lax.rem(unit, vols)
+        away = unit < vols
+        half = jnp.where(away, 1 - side, side)
         unscale = jnp.full((TILE, nx), kap[v], jnp.float32)
-        for step in range(PASSES):
-            def emit(i, value, step=step):
-                if step < PASSES - 1:
-                    field[step % 2, i * TILE : (i + 1) * TILE, :] = value
-                else:
-                    value = value * unscale
-                    send[v, 2 * i] = folded(value, False)
-                    send[v, 2 * i + 1] = folded(value, True)
-
-            advance(getters(v, step), emit)
-
-            if step == 0:
-                @pl.when(v == 0)
-                def _():
-                    pl.semaphore_wait(barrier, n - 1 + has_up.astype(jnp.int32) + has_down.astype(jnp.int32))
-
-                    @pl.when(has_up)
-                    def _():
-                        to_up().start()
-
-                    @pl.when(has_down)
-                    def _():
-                        to_down().start()
-
-        @pl.when(v < vols - 1)
+
+        def keep(buffer):
+            def emit(i, value):
+                field[buffer, (i + 1) * TILE : (i + 2) * TILE, :] = value
+            return emit
+
+        def pack(i, value):
+            value = value * unscale
+            to = half * group + 2 * i
+            send[v, to] = folded(value, False)
+            send[v, to + 1] = folded(value, True)
+
+        base = half * (some - 1)
+        source = start.at[v]
+        get = getters(source, base, some + 3)
+        advance(get[0], get[1:-1], get[-1], keep(0))
+        get = getters(field.at[0], 0, some + 3)
+        advance(get[0], get[1:-1], get[-1], keep(1))
+        get = getters(field.at[1], half, some + 2)
+        advance(get[0], get[1:-1], get[-1], pack)
+
+        @pl.when(unit == 0)
         def _():
-            def whole(to):
+            pl.semaphore_wait(barrier, n - 1 + has_up.astype(jnp.int32) + has_down.astype(jnp.int32))
+
+            @pl.when(has_up)
+            def _():
+                to_up().start()
+
+            @pl.when(has_down)
+            def _():
+                to_down().start()
+
+        def each(first, length, piece):
+            def step(j, _):
+                to = half * group + lax.rem(me + j, group)
+
                 @pl.when(ready(to))
                 def _():
-                    sending(v, 0, depth, v, to).start()
-
-            order(whole)
-
-        @pl.when(v == vols - 1)
+                    sending(v, first, length, piece, to).start()
+
+                return 0
+
+            lax.fori_loop(0, group, step, 0, unroll=group <= 8)
+
+        last = v == vols - 1
+
+        @pl.when(jnp.logical_not(jnp.logical_and(last, away)))
+        def _():
+            each(0, depth, v)
+
+        @pl.when(jnp.logical_and(last, away))
         def _():
             for p in range(parts):
-                def part(to):
-                    @pl.when(ready(to))
-                    def _():
-                        sending(v, p * PACK, PACK, vols - 1 + p, to).start()
-
-                order(part)
+                each(p * PACK, PACK, first_part + p)
 
     def edge(own, other, own_first, v):
         both = [own, other] if own_first else [other, own]
         for step in range(PASSES):
             made = []
-            advance([lambda x=x: x for x in both], lambda i, value: made.append(value))
+            outside = lambda: jnp.zeros_like(own)
+            advance(outside, [lambda x=x: x for x in both], outside, lambda i, value: made.append(value))
             both = made
         return both[0 if own_first else 1] * jnp.full(own.shape, kap[v], jnp.float32)
 
@@ -224,16 +242,25 @@
         @pl.loop(0, vols)
         def _(v):
             other = scaled(beyond[v], v)
-            if own_first:
-                mine = scaled(held[v, rows - PACK : rows, :], v)[TILE:]
-            else:
-                mine = scaled(held[v, :PACK, :], v)[:TILE]
+            at = tiles if own_first else 1
+            mine = start[v, at * TILE : (at + 1) * TILE, :]
             send[v, to] = folded(edge(mine, other, own_first, v), own_first)
+
+        same = side == to // group
 
         @pl.when(me != to)
         def _():
-            for piece in range(len(pieces)):
-                sending(*pieces[piece], piece, to).start()
+            for v in range(vols - 1):
+                sending(v, 0, depth, v, to).start()
+
+            @pl.when(same)
+            def _():
+                sending(vols - 1, 0, depth, near, to).start()
+
+            @pl.when(jnp.logical_not(same))
+            def _():
+                for p in range(parts):
+                    sending(vols - 1, p * PACK, PACK, first_part + p, to).start()
 
     @pl.when(has_up)
     def _():
@@ -262,17 +289,17 @@
 
     for copy in own:
         copy.wait()
-    for piece in range(vols - 1):
+    for piece in range(vols):
         all_of(piece).wait_recv()
 
     block = min(times, 32)
     for p in range(parts):
-        all_of(vols - 1 + p).wait_recv()
+        all_of(first_part + p).wait_recv()
         span = slice(p * PACK, (p + 1) * PACK)
         values = recv[:, span, :].reshape(times * PACK, LANES)
-        for start in range(0, times, block):
-            these = pl.ds(start, block)
-            base = jnp.dot(mix[start * PACK : (start + block) * PACK, :], values, preferred_element_type=jnp.float32)
+        for t in range(0, times, block):
+            these = pl.ds(t, block)
+            base = jnp.dot(mix[t * PACK : (t + block) * PACK, :], values, preferred_element_type=jnp.float32)
             base = base.reshape(block, PACK, LANES)
             got = (recv[these, span, :].astype(jnp.float32) - base) * inverse(base + 0.1)
             ratio[these, span, :] = got
@@ -281,7 +308,7 @@
         slope[1 : times - 1, span] = ((ratio[2:, span] - ratio[: times - 2, span]) * 0.5).astype(jnp.bfloat16)
         slope[times - 1, span] = (ratio[times - 1, span] - ratio[times - 2, span]).astype(jnp.bfloat16)
 
-    for piece in range(len(pieces)):
+    for piece in range(vols + parts):
         all_of(piece).wait_send()
 
     @pl.when(has_up)
@@ -312,7 +339,7 @@
     each = rows // n
     assert planes == 1 and each * 2 == TILE and nx % (2 * LANES) == 0
     depth = each * nx // LANES
-    pieces = vols - 1 + depth // PACK
+    pieces = vols + depth // PACK
     out = jax.ShapeDtypeStruct((times, depth, LANES), jnp.bfloat16)
     f32, bf16 = jnp.float32, jnp.bfloat16
     results = pl.pallas_call(
@@ -326,7 +353,8 @@
             pltpu.VMEM((2, vols * TILE, nx), bf16),
             pltpu.VMEM((2, vols * TILE, nx), bf16),
             pltpu.VMEM((vols, TILE, nx), f32),
-            pltpu.VMEM((2, rows, nx), f32),
+            pltpu.VMEM((vols, rows + 2 * TILE, nx), f32),
+            pltpu.VMEM((2, rows // 2 + 3 * TILE, nx), f32),
             pltpu.VMEM((vols, n, depth, LANES), bf16),
             pltpu.VMEM((times, depth, LANES), bf16),
             pltpu.VMEM((times * PACK, times * PACK), bf16),

time: 16.1 us -> 15.6 us (0.969)
  Pallas kernels: 15.3 us -> 14.9 us
    pallas_call x1, Pallas kernels: 14.5 us -> 14 us  [local(): pl.pallas_call(functools.partial(kernel, n, strips), out_shape=(out, out)...]
where the time goes in v2:
time: 15.6 us; the launch traced here: 15.5 us
  Pallas kernels  14.9 us (96%)
  between operations  0.64 us (4%)
    pallas_call x1, Pallas kernels, local(): pl.pallas_call(functools.partial(kernel, n, strips), out_shape=(out, out)...  14 us
    pallas_call x1, Pallas kernels, local(): pl.pallas_call(leave, out_shape=(out, out), in_specs=[pl.BlockSpec(memory...  0.82 us

profile of v2, /device:TPU:0, one launch (start us, length us, event | category | flops | bytes accessed | tf_op | source)
XLA Modules:
  0.0 15.5 jit_solution(10328653034555608994)
XLA Ops:
  0.6 14.0 %shard_map.41 = (bf16[32,32,128]{2,1,0:T(8,128)(2,1)S(1)}, bf16[32,32,128]{2,1,0:T(8,128)(2,1)S(1)}) custom-call(bf16[2,1,64,1024]{3,2,1,0:T(8,128)(2,1)} %frames.1, f32[2]{0:T(128)} %kappa.1), custom_call_target="tpu_custom_call" | custom-call | flops 200000000 | bytes 1000000 | tf_op jit(solution)/shard_map/pallas_call | solution.py:345
  14.7 0.8 %shard_map.42 = (bf16[32,32,128]{2,1,0:T(8,128)(2,1)}, bf16[32,32,128]{2,1,0:T(8,128)(2,1)}) custom-call(bf16[32,32,128]{2,1,0:T(8,128)(2,1)S(1)} %get-tuple-element.6.dff, bf16[32,32,128]{2,1,0:T(8,128)(2,1)S(1)} %get-tuple-element.7.slope), custom_call_target="tpu_custom_call" | custom-call | bytes 1000000 | tf_op jit(solution)/shard_map/pallas_call | solution.py:374

commit v3 on v2

--- a/solution.py
+++ b/solution.py
@@ -116,15 +116,17 @@
             send_sem=send_sem.at[piece], recv_sem=recv_sem.at[piece],
             device_id={"vol": to}, device_id_type=MESH)
 
+    def joined(to):
+        return pltpu.make_async_remote_copy(
+            src_ref=send.at[:, to], dst_ref=recv.at[pl.ds(me * vols, vols)],
+            send_sem=send_sem.at[near], recv_sem=recv_sem.at[near],
+            device_id={"vol": to}, device_id_type=MESH)
+
     def all_of(piece):
-        count, length = n - 1, depth
-        if piece == near:
-            count = group - 1
-        elif piece >= first_part:
-            count, length = group, PACK
+        count = (group - 1) * vols if piece == near else group
+        these = recv.at[pl.ds(0, count), pl.ds(0, PACK if piece >= first_part else depth)]
         return pltpu.make_async_remote_copy(
-            src_ref=send.at[0, pl.ds(0, count), pl.ds(0, length)], dst_ref=recv.at[pl.ds(0, count), pl.ds(0, length)],
-            send_sem=send_sem.at[piece], recv_sem=recv_sem.at[piece],
+            src_ref=these, dst_ref=these, send_sem=send_sem.at[piece], recv_sem=recv_sem.at[piece],
             device_id={"vol": lax.rem(me + 1, n)}, device_id_type=MESH)
 
     def scaled(block, v):
@@ -149,18 +151,33 @@
         start[v, :TILE, :] = zero
         start[v, (tiles + 1) * TILE :, :] = zero
 
-    load_kappa.wait()
-    for load in loads:
-        load.wait()
+    column = lax.broadcasted_iota(jnp.int32, (PACK, times * PACK), 1)
+    diagonal = column % PACK == lax.broadcasted_iota(jnp.int32, (PACK, times * PACK), 0)
+    source = jnp.where(diagonal, column // PACK, -2 * times - BAND).astype(jnp.float32)
+
+    def weigh(t, _):
+        ahead = jnp.maximum(BAND - t, 0)
+        behind = jnp.maximum(t + BAND + 1 - times, 0)
+        total = (BAND + 1) ** 2 - (ahead * (ahead + 1) + behind * (behind + 1)) // 2
+        share = 1.0 / jnp.full((TILE, LANES), total, jnp.int32).astype(jnp.float32)
+        raw = jnp.maximum(BAND + 1 - jnp.abs(source - t.astype(jnp.float32)), 0.0)
+        raw = raw.reshape(PACK // TILE, TILE, times * PACK)
+        weight = jnp.concatenate(
+            [raw[:, :, c : c + LANES] * share[None] for c in range(0, times * PACK, LANES)], axis=2)
+        mix[pl.ds(pl.multiple_of(t * PACK, PACK), PACK), :] = weight.reshape(PACK, times * PACK).astype(jnp.bfloat16)
+        return 0
+
+    lax.fori_loop(0, times, weigh, 0, unroll=8)
 
     f32 = jnp.float32
-    rim[1] = jnp.concatenate(
-        [held[v, :PACK, :].astype(f32)[:TILE] for v in range(vols)], axis=0).astype(jnp.bfloat16)
-    rim[0] = jnp.concatenate(
-        [held[v, rows - PACK :, :].astype(f32)[TILE:] for v in range(vols)], axis=0).astype(jnp.bfloat16)
-    for v in range(vols):
+
+    def enter(v):
+        loads[v].wait()
         for i in range(rows // PACK):
             start[v, TILE + i * PACK : TILE + (i + 1) * PACK, :] = scaled(held[v, i * PACK : (i + 1) * PACK, :], v)
+
+    load_kappa.wait()
+    enter(0)
 
     @pl.loop(0, 2 * vols)
     def _(unit):
@@ -191,6 +208,12 @@
 
         @pl.when(unit == 0)
         def _():
+            for w in range(1, vols):
+                enter(w)
+            rim[1] = jnp.concatenate(
+                [held[w, :PACK, :].astype(f32)[:TILE] for w in range(vols)], axis=0).astype(jnp.bfloat16)
+            rim[0] = jnp.concatenate(
+                [held[w, rows - PACK :, :].astype(f32)[TILE:] for w in range(vols)], axis=0).astype(jnp.bfloat16)
             pl.semaphore_wait(barrier, n - 1 + has_up.astype(jnp.int32) + has_down.astype(jnp.int32))
 
             @pl.when(has_up)
@@ -201,13 +224,13 @@
             def _():
                 to_down().start()
 
-        def each(first, length, piece):
+        def each(copy):
             def step(j, _):
                 to = half * group + lax.rem(me + j, group)
 
                 @pl.when(ready(to))
                 def _():
-                    sending(v, first, length, piece, to).start()
+                    copy(to).start()
 
                 return 0
 
@@ -215,14 +238,18 @@
 
         last = v == vols - 1
 
-        @pl.when(jnp.logical_not(jnp.logical_and(last, away)))
-        def _():
-            each(0, depth, v)
-
-        @pl.when(jnp.logical_and(last, away))
+        @pl.when(jnp.logical_and(away, jnp.logical_not(last)))
+        def _():
+            each(lambda to: sending(v, 0, depth, v, to))
+
+        @pl.when(jnp.logical_and(away, last))
         def _():
             for p in range(parts):
-                each(p * PACK, PACK, first_part + p)
+                each(lambda to: sending(v, p * PACK, PACK, first_part + p, to))
+
+        @pl.when(jnp.logical_and(last, jnp.logical_not(away)))
+        def _():
+            each(joined)
 
     def edge(own, other, own_first, v):
         both = [own, other] if own_first else [other, own]
@@ -248,19 +275,16 @@
 
         same = side == to // group
 
-        @pl.when(me != to)
+        @pl.when(jnp.logical_and(same, me != to))
+        def _():
+            joined(to).start()
+
+        @pl.when(jnp.logical_not(same))
         def _():
             for v in range(vols - 1):
                 sending(v, 0, depth, v, to).start()
-
-            @pl.when(same)
-            def _():
-                sending(vols - 1, 0, depth, near, to).start()
-
-            @pl.when(jnp.logical_not(same))
-            def _():
-                for p in range(parts):
-                    sending(vols - 1, p * PACK, PACK, first_part + p, to).start()
+            for p in range(parts):
+                sending(vols - 1, p * PACK, PACK, first_part + p, to).start()
 
     @pl.when(has_up)
     def _():
@@ -273,19 +297,6 @@
     own = [pltpu.make_async_copy(send.at[v, me], recv.at[me * vols + v], own_sem.at[v]) for v in range(vols)]
     for copy in own:
         copy.start()
-
-    column = lax.broadcasted_iota(jnp.int32, (PACK, times * PACK), 1)
-    diagonal = column % PACK == lax.broadcasted_iota(jnp.int32, (PACK, times * PACK), 0)
-    source = column // PACK
-
-    @pl.loop(0, times)
-    def _(t):
-        ahead = jnp.maximum(BAND - t, 0)
-        behind = jnp.maximum(t + BAND + 1 - times, 0)
-        total = (BAND + 1) ** 2 - (ahead * (ahead + 1) + behind * (behind + 1)) // 2
-        raw = jnp.maximum(BAND + 1 - jnp.abs(source - t), 0).astype(jnp.float32)
-        weight = raw / jnp.full(raw.shape, total, jnp.int32).astype(jnp.float32)
-        mix[pl.ds(pl.multiple_of(t * PACK, PACK), PACK), :] = jnp.where(diagonal, weight, 0.0).astype(jnp.bfloat16)
 
     for copy in own:
         copy.wait()
@@ -321,11 +332,11 @@
 
 
 def leave(dff, slope, dff_out, slope_out, sem):
-    half = dff.shape[0] // 2
+    part = dff.shape[0] // 4
     copies = [
-        pltpu.make_async_copy(source.at[pl.ds(h * half, half)], target.at[pl.ds(h * half, half)], sem.at[k, h])
+        pltpu.make_async_copy(source.at[pl.ds(h * part, part)], target.at[pl.ds(h * part, part)], sem.at[k, h])
         for k, (source, target) in enumerate(((dff, dff_out), (slope, slope_out)))
-        for h in range(2)
+        for h in range(4)
     ]
     for copy in copies:
         copy.start()
@@ -376,7 +387,7 @@
         out_shape=(out, out),
         in_specs=[pl.BlockSpec(memory_space=pl.ANY)] * 2,
         out_specs=(pl.BlockSpec(memory_space=pltpu.HBM),) * 2,
-        scratch_shapes=[pltpu.SemaphoreType.DMA((2, 2))],
+        scratch_shapes=[pltpu.SemaphoreType.DMA((2, 4))],
         compiler_params=pltpu.CompilerParams(vmem_limit_bytes=2 * 1024 * 1024),
         cost_estimate=pl.CostEstimate(flops=0, bytes_accessed=1_000_000, transcendentals=0),
     )(*[pltpu.with_memory_space_constraint(x, pltpu.VMEM) for x in results])

time: 15.6 us -> 15.7 us (level)
  no operation moved by 1% of the time
where the time goes in v3:
time: 15.7 us; the launch traced here: 15.5 us
  Pallas kernels  14.9 us (95%)
  between operations  0.64 us (4%)
    pallas_call x1, Pallas kernels, local(): pl.pallas_call(functools.partial(kernel, n, strips), out_shape=(out, out)...  14 us
    pallas_call x1, Pallas kernels, local(): pl.pallas_call(leave, out_shape=(out, out), in_specs=[pl.BlockSpec(memory...  0.85 us

profile of v3, /device:TPU:0, one launch (start us, length us, event | category | flops | bytes accessed | tf_op | source)
XLA Modules:
  0.0 15.5 jit_solution(15133833893383107232)
XLA Ops:
  0.6 14.0 %shard_map.41 = (bf16[32,32,128]{2,1,0:T(8,128)(2,1)S(1)}, bf16[32,32,128]{2,1,0:T(8,128)(2,1)S(1)}) custom-call(bf16[2,1,64,1024]{3,2,1,0:T(8,128)(2,1)} %frames.1, f32[2]{0:T(128)} %kappa.1), custom_call_target="tpu_custom_call" | custom-call | flops 200000000 | bytes 1000000 | tf_op jit(solution)/shard_map/pallas_call | solution.py:356
  14.7 0.9 %shard_map.42 = (bf16[32,32,128]{2,1,0:T(8,128)(2,1)}, bf16[32,32,128]{2,1,0:T(8,128)(2,1)}) custom-call(bf16[32,32,128]{2,1,0:T(8,128)(2,1)S(1)} %get-tuple-element.6.dff, bf16[32,32,128]{2,1,0:T(8,128)(2,1)S(1)} %get-tuple-element.7.slope), custom_call_target="tpu_custom_call" | custom-call | bytes 1000000 | tf_op jit(solution)/shard_map/pallas_call | solution.py:385

commit v4 on v3

--- a/solution.py
+++ b/solution.py
@@ -123,8 +123,9 @@
             device_id={"vol": to}, device_id_type=MESH)
 
     def all_of(piece):
-        count = (group - 1) * vols if piece == near else group
-        these = recv.at[pl.ds(0, count), pl.ds(0, PACK if piece >= first_part else depth)]
+        last = not isinstance(piece, int) or piece >= first_part
+        count = (group - 1) * vols if not last and piece == near else group
+        these = recv.at[pl.ds(0, count), pl.ds(0, PACK if last else depth)]
         return pltpu.make_async_remote_copy(
             src_ref=these, dst_ref=these, send_sem=send_sem.at[piece], recv_sem=recv_sem.at[piece],
             device_id={"vol": lax.rem(me + 1, n)}, device_id_type=MESH)
@@ -167,7 +168,7 @@
         mix[pl.ds(pl.multiple_of(t * PACK, PACK), PACK), :] = weight.reshape(PACK, times * PACK).astype(jnp.bfloat16)
         return 0
 
-    lax.fori_loop(0, times, weigh, 0, unroll=8)
+    lax.fori_loop(0, times, weigh, 0, unroll=4)
 
     f32 = jnp.float32
 
@@ -186,25 +187,26 @@
         half = jnp.where(away, 1 - side, side)
         unscale = jnp.full((TILE, nx), kap[v], jnp.float32)
 
-        def keep(buffer):
-            def emit(i, value):
-                field[buffer, (i + 1) * TILE : (i + 2) * TILE, :] = value
-            return emit
-
-        def pack(i, value):
-            value = value * unscale
+        base = pl.multiple_of((half * (some - 1) + 1) * TILE, TILE)
+        span = (some + 1) * TILE
+        field[0, TILE : TILE + span, :] = start[v, pl.ds(base, span), :]
+
+        @pl.loop(0, PASSES)
+        def _(step):
+            old, new = field.at[step % 2], field.at[(step + 1) % 2]
+
+            def keep(i, value):
+                new[(i + 1) * TILE : (i + 2) * TILE, :] = value
+
+            get = getters(old, 0, some + 3)
+            advance(get[0], get[1:-1], get[-1], keep)
+
+        @pl.loop(0, some)
+        def _(i):
+            value = tile(field.at[PASSES % 2], half + 1 + i) * unscale
             to = half * group + 2 * i
             send[v, to] = folded(value, False)
             send[v, to + 1] = folded(value, True)
-
-        base = half * (some - 1)
-        source = start.at[v]
-        get = getters(source, base, some + 3)
-        advance(get[0], get[1:-1], get[-1], keep(0))
-        get = getters(field.at[0], 0, some + 3)
-        advance(get[0], get[1:-1], get[-1], keep(1))
-        get = getters(field.at[1], half, some + 2)
-        advance(get[0], get[1:-1], get[-1], pack)
 
         @pl.when(unit == 0)
         def _():
@@ -252,12 +254,13 @@
             each(joined)
 
     def edge(own, other, own_first, v):
-        both = [own, other] if own_first else [other, own]
-        for step in range(PASSES):
+        def step(_, both):
             made = []
             outside = lambda: jnp.zeros_like(own)
             advance(outside, [lambda x=x: x for x in both], outside, lambda i, value: made.append(value))
-            both = made
+            return tuple(made)
+
+        both = lax.fori_loop(0, PASSES, step, (own, other) if own_first else (other, own))
         return both[0 if own_first else 1] * jnp.full(own.shape, kap[v], jnp.float32)
 
     def edges(to, copy, which, own_first):
@@ -303,21 +306,34 @@
     for piece in range(vols):
         all_of(piece).wait_recv()
 
-    block = min(times, 32)
-    for p in range(parts):
+    block = 8
+    ratio[0] = jnp.zeros(ratio.shape[1:], f32)
+    ratio[times + 1] = jnp.zeros(ratio.shape[1:], f32)
+
+    @pl.loop(0, parts)
+    def _(p):
         all_of(first_part + p).wait_recv()
-        span = slice(p * PACK, (p + 1) * PACK)
+        span = pl.ds(pl.multiple_of(p * PACK, PACK), PACK)
         values = recv[:, span, :].reshape(times * PACK, LANES)
-        for t in range(0, times, block):
-            these = pl.ds(t, block)
-            base = jnp.dot(mix[t * PACK : (t + block) * PACK, :], values, preferred_element_type=jnp.float32)
+
+        @pl.loop(0, times // block)
+        def _(b):
+            these = pl.ds(b * block, block)
+            lines = pl.ds(pl.multiple_of(b * block * PACK, block * PACK), block * PACK)
+            base = jnp.dot(mix[lines, :], values, preferred_element_type=jnp.float32)
             base = base.reshape(block, PACK, LANES)
             got = (recv[these, span, :].astype(jnp.float32) - base) * inverse(base + 0.1)
-            ratio[these, span, :] = got
+            ratio[pl.ds(b * block + 1, block), span, :] = got
             dff[these, span, :] = got.astype(jnp.bfloat16)
-        slope[0, span] = (ratio[1, span] - ratio[0, span]).astype(jnp.bfloat16)
-        slope[1 : times - 1, span] = ((ratio[2:, span] - ratio[: times - 2, span]) * 0.5).astype(jnp.bfloat16)
-        slope[times - 1, span] = (ratio[times - 1, span] - ratio[times - 2, span]).astype(jnp.bfloat16)
+
+        @pl.loop(0, times // block)
+        def _(b):
+            t = b * block
+            change = (ratio[pl.ds(t + 2, block), span, :] - ratio[pl.ds(t, block), span, :]) * 0.5
+            slope[pl.ds(t, block), span, :] = change.astype(jnp.bfloat16)
+
+        slope[0, span, :] = (ratio[2, span, :] - ratio[1, span, :]).astype(jnp.bfloat16)
+        slope[times - 1, span, :] = (ratio[times, span, :] - ratio[times - 1, span, :]).astype(jnp.bfloat16)
 
     for piece in range(vols + parts):
         all_of(piece).wait_send()
@@ -369,7 +385,7 @@
             pltpu.VMEM((vols, n, depth, LANES), bf16),
             pltpu.VMEM((times, depth, LANES), bf16),
             pltpu.VMEM((times * PACK, times * PACK), bf16),
-            pltpu.VMEM((times, depth, LANES), f32),
+            pltpu.VMEM((times + 2, depth, LANES), f32),
             pltpu.SemaphoreType.DMA((vols + 1,)),
             pltpu.SemaphoreType.DMA((2,)),
             pltpu.SemaphoreType.DMA((2,)),

time: 15.7 us -> 16.4 us (1.045)
  Pallas kernels: 14.9 us -> 15.6 us
    pallas_call x1, Pallas kernels: 14 us -> 14.8 us  [local(): pl.pallas_call(functools.partial(kernel, n, strips), out_shape=(out, out)...]
where the time goes in v4:
time: 16.4 us; the launch traced here: 16.3 us
  Pallas kernels  15.6 us (95%)
  between operations  0.64 us (4%)
    pallas_call x1, Pallas kernels, local(): pl.pallas_call(functools.partial(kernel, n, strips), out_shape=(out, out)...  14.8 us
    pallas_call x1, Pallas kernels, local(): pl.pallas_call(leave, out_shape=(out, out), in_specs=[pl.BlockSpec(memory...  0.85 us

profile of v4, /device:TPU:0, one launch (start us, length us, event | category | flops | bytes accessed | tf_op | source)
XLA Modules:
  0.0 16.3 jit_solution(8847080665323346270)
XLA Ops:
  0.6 14.8 %shard_map.41 = (bf16[32,32,128]{2,1,0:T(8,128)(2,1)S(1)}, bf16[32,32,128]{2,1,0:T(8,128)(2,1)S(1)}) custom-call(bf16[2,1,64,1024]{3,2,1,0:T(8,128)(2,1)} %frames.1, f32[2]{0:T(128)} %kappa.1), custom_call_target="tpu_custom_call" | custom-call | flops 200000000 | bytes 1000000 | tf_op jit(solution)/shard_map/pallas_call | solution.py:372
  15.4 0.9 %shard_map.42 = (bf16[32,32,128]{2,1,0:T(8,128)(2,1)}, bf16[32,32,128]{2,1,0:T(8,128)(2,1)}) custom-call(bf16[32,32,128]{2,1,0:T(8,128)(2,1)S(1)} %get-tuple-element.6.dff, bf16[32,32,128]{2,1,0:T(8,128)(2,1)S(1)} %get-tuple-element.7.slope), custom_call_target="tpu_custom_call" | custom-call | bytes 1000000 | tf_op jit(solution)/shard_map/pallas_call | solution.py:401

commit v5 on v3

--- a/solution.py
+++ b/solution.py
@@ -151,6 +151,137 @@
         start[v, :TILE, :] = zero
         start[v, (tiles + 1) * TILE :, :] = zero
 
+    f32 = jnp.float32
+
+    def enter(v):
+        loads[v].wait()
+        for i in range(rows // PACK):
+            start[v, TILE + i * PACK : TILE + (i + 1) * PACK, :] = scaled(held[v, i * PACK : (i + 1) * PACK, :], v)
+
+    load_kappa.wait()
+    enter(0)
+
+    @pl.loop(0, 2 * vols)
+    def _(unit):
+        v = lax.rem(unit, vols)
+        away = unit < vols
+        half = jnp.where(away, 1 - side, side)
+        unscale = jnp.full((TILE, nx), kap[v], jnp.float32)
+
+        def keep(buffer):
+            def emit(i, value):
+                field[buffer, (i + 1) * TILE : (i + 2) * TILE, :] = value
+            return emit
+
+        def pack(i, value):
+            value = value * unscale
+            to = half * group + 2 * i
+            send[v, to] = folded(value, False)
+            send[v, to + 1] = folded(value, True)
+
+        base = half * (some - 1)
+        source = start.at[v]
+        get = getters(source, base, some + 3)
+        advance(get[0], get[1:-1], get[-1], keep(0))
+        get = getters(field.at[0], 0, some + 3)
+        advance(get[0], get[1:-1], get[-1], keep(1))
+        get = getters(field.at[1], half, some + 2)
+        advance(get[0], get[1:-1], get[-1], pack)
+
+        @pl.when(unit == 0)
+        def _():
+            pl.semaphore_wait(barrier, n - 1 + has_up.astype(jnp.int32) + has_down.astype(jnp.int32))
+
+        def each(copy):
+            def step(j, _):
+                to = half * group + lax.rem(me + j, group)
+
+                @pl.when(ready(to))
+                def _():
+                    copy(to).start()
+
+                return 0
+
+            lax.fori_loop(0, group, step, 0, unroll=group <= 8)
+
+        last = v == vols - 1
+
+        @pl.when(jnp.logical_and(away, jnp.logical_not(last)))
+        def _():
+            each(lambda to: sending(v, 0, depth, v, to))
+
+        @pl.when(jnp.logical_and(away, last))
+        def _():
+            for p in range(parts):
+                each(lambda to: sending(v, p * PACK, PACK, first_part + p, to))
+
+        @pl.when(jnp.logical_and(last, jnp.logical_not(away)))
+        def _():
+            each(joined)
+
+        @pl.when(unit == 0)
+        def _():
+            for w in range(1, vols):
+                enter(w)
+            rim[1] = jnp.concatenate(
+                [held[w, :PACK, :].astype(f32)[:TILE] for w in range(vols)], axis=0).astype(jnp.bfloat16)
+            rim[0] = jnp.concatenate(
+                [held[w, rows - PACK :, :].astype(f32)[TILE:] for w in range(vols)], axis=0).astype(jnp.bfloat16)
+            @pl.when(has_up)
+            def _():
+                to_up().start()
+
+            @pl.when(has_down)
+            def _():
+                to_down().start()
+
+    def edge(own, other, own_first, v):
+        both = [own, other] if own_first else [other, own]
+        for step in range(PASSES):
+            made = []
+            outside = lambda: jnp.zeros_like(own)
+            advance(outside, [lambda x=x: x for x in both], outside, lambda i, value: made.append(value))
+            both = made
+        return both[0 if own_first else 1] * jnp.full(own.shape, kap[v], jnp.float32)
+
+    def edges(to, copy, which, own_first):
+        copy.wait_recv()
+        got = halo[which].astype(f32)
+        for v in range(vols):
+            beyond[v] = got[v * TILE : (v + 1) * TILE]
+
+        @pl.loop(0, vols)
+        def _(v):
+            other = scaled(beyond[v], v)
+            at = tiles if own_first else 1
+            mine = start[v, at * TILE : (at + 1) * TILE, :]
+            send[v, to] = folded(edge(mine, other, own_first, v), own_first)
+
+        same = side == to // group
+
+        @pl.when(jnp.logical_and(same, me != to))
+        def _():
+            joined(to).start()
+
+        @pl.when(jnp.logical_not(same))
+        def _():
+            for v in range(vols - 1):
+                sending(v, 0, depth, v, to).start()
+            for p in range(parts):
+                sending(vols - 1, p * PACK, PACK, first_part + p, to).start()
+
+    @pl.when(has_up)
+    def _():
+        edges(0, to_down(), 0, False)
+
+    @pl.when(has_down)
+    def _():
+        edges(n - 1, to_up(), 1, True)
+
+    own = [pltpu.make_async_copy(send.at[v, me], recv.at[me * vols + v], own_sem.at[v]) for v in range(vols)]
+    for copy in own:
+        copy.start()
+
     column = lax.broadcasted_iota(jnp.int32, (PACK, times * PACK), 1)
     diagonal = column % PACK == lax.broadcasted_iota(jnp.int32, (PACK, times * PACK), 0)
     source = jnp.where(diagonal, column // PACK, -2 * times - BAND).astype(jnp.float32)
@@ -168,135 +299,6 @@
         return 0
 
     lax.fori_loop(0, times, weigh, 0, unroll=8)
-
-    f32 = jnp.float32
-
-    def enter(v):
-        loads[v].wait()
-        for i in range(rows // PACK):
-            start[v, TILE + i * PACK : TILE + (i + 1) * PACK, :] = scaled(held[v, i * PACK : (i + 1) * PACK, :], v)
-
-    load_kappa.wait()
-    enter(0)
-
-    @pl.loop(0, 2 * vols)
-    def _(unit):
-        v = lax.rem(unit, vols)
-        away = unit < vols
-        half = jnp.where(away, 1 - side, side)
-        unscale = jnp.full((TILE, nx), kap[v], jnp.float32)
-
-        def keep(buffer):
-            def emit(i, value):
-                field[buffer, (i + 1) * TILE : (i + 2) * TILE, :] = value
-            return emit
-
-        def pack(i, value):
-            value = value * unscale
-            to = half * group + 2 * i
-            send[v, to] = folded(value, False)
-            send[v, to + 1] = folded(value, True)
-
-        base = half * (some - 1)
-        source = start.at[v]
-        get = getters(source, base, some + 3)
-        advance(get[0], get[1:-1], get[-1], keep(0))
-        get = getters(field.at[0], 0, some + 3)
-        advance(get[0], get[1:-1], get[-1], keep(1))
-        get = getters(field.at[1], half, some + 2)
-        advance(get[0], get[1:-1], get[-1], pack)
-
-        @pl.when(unit == 0)
-        def _():
-            for w in range(1, vols):
-                enter(w)
-            rim[1] = jnp.concatenate(
-                [held[w, :PACK, :].astype(f32)[:TILE] for w in range(vols)], axis=0).astype(jnp.bfloat16)
-            rim[0] = jnp.concatenate(
-                [held[w, rows - PACK :, :].astype(f32)[TILE:] for w in range(vols)], axis=0).astype(jnp.bfloat16)
-            pl.semaphore_wait(barrier, n - 1 + has_up.astype(jnp.int32) + has_down.astype(jnp.int32))
-
-            @pl.when(has_up)
-            def _():
-                to_up().start()
-
-            @pl.when(has_down)
-            def _():
-                to_down().start()
-
-        def each(copy):
-            def step(j, _):
-                to = half * group + lax.rem(me + j, group)
-
-                @pl.when(ready(to))
-                def _():
-                    copy(to).start()
-
-                return 0
-
-            lax.fori_loop(0, group, step, 0, unroll=group <= 8)
-
-        last = v == vols - 1
-
-        @pl.when(jnp.logical_and(away, jnp.logical_not(last)))
-        def _():
-            each(lambda to: sending(v, 0, depth, v, to))
-
-        @pl.when(jnp.logical_and(away, last))
-        def _():
-            for p in range(parts):
-                each(lambda to: sending(v, p * PACK, PACK, first_part + p, to))
-
-        @pl.when(jnp.logical_and(last, jnp.logical_not(away)))
-        def _():
-            each(joined)
-
-    def edge(own, other, own_first, v):
-        both = [own, other] if own_first else [other, own]
-        for step in range(PASSES):
-            made = []
-            outside = lambda: jnp.zeros_like(own)
-            advance(outside, [lambda x=x: x for x in both], outside, lambda i, value: made.append(value))
-            both = made
-        return both[0 if own_first else 1] * jnp.full(own.shape, kap[v], jnp.float32)
-
-    def edges(to, copy, which, own_first):
-        copy.wait_recv()
-        got = halo[which].astype(f32)
-        for v in range(vols):
-            beyond[v] = got[v * TILE : (v + 1) * TILE]
-
-        @pl.loop(0, vols)
-        def _(v):
-            other = scaled(beyond[v], v)
-            at = tiles if own_first else 1
-            mine = start[v, at * TILE : (at + 1) * TILE, :]
-            send[v, to] = folded(edge(mine, other, own_first, v), own_first)
-
-        same = side == to // group
-
-        @pl.when(jnp.logical_and(same, me != to))
-        def _():
-            joined(to).start()
-
-        @pl.when(jnp.logical_not(same))
-        def _():
-            for v in range(vols - 1):
-                sending(v, 0, depth, v, to).start()
-            for p in range(parts):
-                sending(vols - 1, p * PACK, PACK, first_part + p, to).start()
-
-    @pl.when(has_up)
-    def _():
-        edges(0, to_down(), 0, False)
-
-    @pl.when(has_down)
-    def _():
-        edges(n - 1, to_up(), 1, True)
-
-    own = [pltpu.make_async_copy(send.at[v, me], recv.at[me * vols + v], own_sem.at[v]) for v in range(vols)]
-    for copy in own:
-        copy.start()
 
     for copy in own:
         copy.wait()
@@ -332,11 +334,11 @@
 
 
 def leave(dff, slope, dff_out, slope_out, sem):
-    part = dff.shape[0] // 4
+    part = dff.shape[0] // 2
     copies = [
         pltpu.make_async_copy(source.at[pl.ds(h * part, part)], target.at[pl.ds(h * part, part)], sem.at[k, h])
         for k, (source, target) in enumerate(((dff, dff_out), (slope, slope_out)))
-        for h in range(4)
+        for h in range(2)
     ]
     for copy in copies:
         copy.start()
@@ -387,7 +389,7 @@
         out_shape=(out, out),
         in_specs=[pl.BlockSpec(memory_space=pl.ANY)] * 2,
         out_specs=(pl.BlockSpec(memory_space=pltpu.HBM),) * 2,
-        scratch_shapes=[pltpu.SemaphoreType.DMA((2, 4))],
+        scratch_shapes=[pltpu.SemaphoreType.DMA((2, 2))],
         compiler_params=pltpu.CompilerParams(vmem_limit_bytes=2 * 1024 * 1024),
         cost_estimate=pl.CostEstimate(flops=0, bytes_accessed=1_000_000, transcendentals=0),
     )(*[pltpu.with_memory_space_constraint(x, pltpu.VMEM) for x in results])

time: 15.7 us -> 15.6 us (level)
  no operation moved by 1% of the time
where the time goes in v5:
time: 15.6 us; the launch traced here: 15.5 us
  Pallas kernels  14.9 us (96%)
  between operations  0.64 us (4%)
    pallas_call x1, Pallas kernels, local(): pl.pallas_call(functools.partial(kernel, n, strips), out_shape=(out, out)...  14 us
    pallas_call x1, Pallas kernels, local(): pl.pallas_call(leave, out_shape=(out, out), in_specs=[pl.BlockSpec(memory...  0.82 us

profile of v5, /device:TPU:0, one launch (start us, length us, event | category | flops | bytes accessed | tf_op | source)
XLA Modules:
  0.0 15.5 jit_solution(3676088143813364349)
XLA Ops:
  0.6 14.0 %shard_map.41 = (bf16[32,32,128]{2,1,0:T(8,128)(2,1)S(1)}, bf16[32,32,128]{2,1,0:T(8,128)(2,1)S(1)}) custom-call(bf16[2,1,64,1024]{3,2,1,0:T(8,128)(2,1)} %frames.1, f32[2]{0:T(128)} %kappa.1), custom_call_target="tpu_custom_call" | custom-call | flops 200000000 | bytes 1000000 | tf_op jit(solution)/shard_map/pallas_call | solution.py:358
  14.7 0.8 %shard_map.42 = (bf16[32,32,128]{2,1,0:T(8,128)(2,1)}, bf16[32,32,128]{2,1,0:T(8,128)(2,1)}) custom-call(bf16[32,32,128]{2,1,0:T(8,128)(2,1)S(1)} %get-tuple-element.6.dff, bf16[32,32,128]{2,1,0:T(8,128)(2,1)S(1)} %get-tuple-element.7.slope), custom_call_target="tpu_custom_call" | custom-call | bytes 1000000 | tf_op jit(solution)/shard_map/pallas_call | solution.py:387

commit v6 on v5

--- a/solution.py
+++ b/solution.py
@@ -66,7 +66,7 @@
 
 
 def kernel(n, strips, frames, kappa, dff, slope, held, kap, rim, halo, beyond, start, field, send, recv, mix, ratio,
-           load_sem, halo_send, halo_recv, send_sem, recv_sem, own_sem):
+           load_sem, halo_send, halo_recv, send_sem, recv_sem, own_sem, near_sem):
     vols, _, rows, nx = frames.shape
     times, depth, _ = recv.shape
     tiles = rows // TILE
@@ -83,9 +83,13 @@
 
     barrier = pltpu.get_barrier_semaphore()
 
-    @pl.loop(1, n)
+    group = n // 2
+    side = me // group
+
+    @pl.loop(0, group)
     def _(k):
-        pl.semaphore_signal(barrier, inc=1, device_id={"vol": lax.rem(me + k, n)}, device_id_type=MESH)
+        to = (1 - side) * group + lax.rem(me + k, group)
+        pl.semaphore_signal(barrier, inc=1, device_id={"vol": to}, device_id_type=MESH)
 
     @pl.when(has_up)
     def _():
@@ -106,8 +110,6 @@
             device_id={"strip": strip + 1}, device_id_type=MESH)
 
     parts = depth // PACK
-    group = n // 2
-    side = me // group
     near, first_part = vols - 1, vols
 
     def sending(v, start, length, piece, to):
@@ -190,7 +192,8 @@
 
         @pl.when(unit == 0)
         def _():
-            pl.semaphore_wait(barrier, n - 1 + has_up.astype(jnp.int32) + has_down.astype(jnp.int32))
+            pl.semaphore_wait(barrier, group + has_up.astype(jnp.int32) + has_down.astype(jnp.int32))
+            pl.semaphore_signal(near_sem, inc=1, device_id={"vol": lax.rem(me + group, n)}, device_id_type=MESH)
 
         def each(copy):
             def step(j, _):
@@ -217,6 +220,7 @@
 
         @pl.when(jnp.logical_and(last, jnp.logical_not(away)))
         def _():
+            pl.semaphore_wait(near_sem, 1)
             each(joined)
 
         @pl.when(unit == 0)
@@ -378,6 +382,7 @@
             pltpu.SemaphoreType.DMA((pieces,)),
             pltpu.SemaphoreType.DMA((pieces,)),
             pltpu.SemaphoreType.DMA((vols,)),
+            pltpu.SemaphoreType.REGULAR,
         ],
         compiler_params=pltpu.CompilerParams(
             collective_id=0, has_side_effects=True, vmem_limit_bytes=40 * 1024 * 1024),

time: 15.6 us -> 15.3 us (0.981)
  Pallas kernels: 14.9 us -> 14.6 us
    pallas_call x1, Pallas kernels: 14 us -> 13.7 us  [local(): pl.pallas_call(functools.partial(kernel, n, strips), out_shape=(out, out)...]
where the time goes in v6:
time: 15.3 us; the launch traced here: 15.2 us
  Pallas kernels  14.6 us (95%)
  between operations  0.64 us (4%)
    pallas_call x1, Pallas kernels, local(): pl.pallas_call(functools.partial(kernel, n, strips), out_shape=(out, out)...  13.7 us
    pallas_call x1, Pallas kernels, local(): pl.pallas_call(leave, out_shape=(out, out), in_specs=[pl.BlockSpec(memory...  0.82 us

profile of v6, /device:TPU:0, one launch (start us, length us, event | category | flops | bytes accessed | tf_op | source)
XLA Modules:
  0.0 15.2 jit_solution(17197613587717860466)
XLA Ops:
  0.6 13.7 %shard_map.41 = (bf16[32,32,128]{2,1,0:T(8,128)(2,1)S(1)}, bf16[32,32,128]{2,1,0:T(8,128)(2,1)S(1)}) custom-call(bf16[2,1,64,1024]{3,2,1,0:T(8,128)(2,1)} %frames.1, f32[2]{0:T(128)} %kappa.1), custom_call_target="tpu_custom_call" | custom-call | flops 200000000 | bytes 1000000 | tf_op jit(solution)/shard_map/pallas_call | solution.py:362
  14.4 0.8 %shard_map.42 = (bf16[32,32,128]{2,1,0:T(8,128)(2,1)}, bf16[32,32,128]{2,1,0:T(8,128)(2,1)}) custom-call(bf16[32,32,128]{2,1,0:T(8,128)(2,1)S(1)} %get-tuple-element.6.dff, bf16[32,32,128]{2,1,0:T(8,128)(2,1)S(1)} %get-tuple-element.7.slope), custom_call_target="tpu_custom_call" | custom-call | bytes 1000000 | tf_op jit(solution)/shard_map/pallas_call | solution.py:392
